TPU v7x, 512 devices: a whole 4x4x16 slice. The times are simulated.
512 devices in a mesh: blk: 32 (over z, core), grp: 16 (over y, x).
Axes of the slice: x: 4, y: 4, z: 16, core: 2. Of those that a mesh axis runs over, the one named last changes fastest.
Arguments:
- labels: float32 [16, 16384, 256], P('grp', 'blk'), may hold values from 0.1 to 10
- tiles: bfloat16 [16, 128, 16, 128, 128], P('grp', 'blk'), may hold values from 0.001 to 1
- tile_cols: int32 [16, 128, 16], P('grp', 'blk'), may hold values from 0 to 23
- tile_count: int32 [16, 128], P('grp', 'blk'), may hold values from 4 to 16
- send_blocks: int32 [16, 32, 16, 1], P('grp', 'blk'), may hold values from 0 to 3
Outputs:
- spread: float32 [16, 16384, 256], P('grp', 'blk')
All inputs are finite; a program needn't handle non-finite values.
Results may differ from a plain program's by a relative error of at most 0.0006.
Values may be sent and summed in bfloat16 or wider, within the bound.
A program may use at most 64 MiB of HBM per device.

v0:
```python
import jax
import jax.numpy as jnp
from jax import lax
from jax.sharding import PartitionSpec as P

HB = 2
ITERS = 3


def with_halo(block, sides, width):
    for axis, dim in sides:
        count = lax.axis_size(axis)
        forward = [(i, i + 1) for i in range(count - 1)]
        backward = [(target, source) for source, target in forward]
        low = lax.ppermute(
            lax.slice_in_dim(block, block.shape[dim] - width, None, axis=dim), axis, forward
        )
        high = lax.ppermute(lax.slice_in_dim(block, 0, width, axis=dim), axis, backward)
        block = jnp.concatenate([low, block, high], axis=dim)
    return block


def on_device(labels, tiles, tile_cols, tile_count, send_blocks):
    n_rows = tiles.shape[1]
    kmax = tiles.shape[2]
    bsize = tiles.shape[3]
    classes = labels.shape[2]
    n_bands = lax.axis_size("grp")
    slots = jnp.arange(kmax, dtype=jnp.int32)
    valid = slots[None, :] < tile_count[0][:, None]
    row_sums = jnp.sum(tiles[0], axis=-1, dtype=jnp.float32)
    deg = jnp.sum(jnp.where(valid[..., None], row_sums, 0.0), axis=1)
    scale = lax.rsqrt(deg).reshape(n_rows * bsize)
    anchor = labels[0]
    picks = send_blocks[0, 0]
    band_ids = jnp.arange(n_bands, dtype=jnp.int32)
    arrived = lax.all_to_all(picks, "grp", split_axis=0, concat_axis=0, tiled=True)
    field = anchor
    for step in range(ITERS):
        scaled = (scale[:, None] * field).astype(jnp.bfloat16)
        padded = with_halo(scaled, (("blk", 0),), HB * bsize)
        local = padded.reshape(n_rows + 2 * HB, bsize, classes)
        own_blocks = scaled.reshape(n_rows, bsize, classes)
        copies = lax.all_gather(own_blocks[None], "grp", axis=0, tiled=True)
        cross = copies[band_ids[:, None], arrived]
        ext = jnp.concatenate([local, cross.reshape(-1, bsize, classes)], axis=0)
        chosen = jnp.where(valid[..., None, None], ext[tile_cols[0]], jnp.zeros((), jnp.bfloat16))
        summed = jnp.einsum("rkij,rkjc->ric", tiles[0], chosen, preferred_element_type=jnp.float32)
        summed = summed.reshape(n_rows * bsize, classes)
        update = 0.9 * scale[:, None] * summed + 0.1 * anchor
        field = update / jnp.mean(update, axis=-1, keepdims=True)
    return field[None]


def solution(mesh):
    return jax.shard_map(
        on_device,
        mesh=mesh,
        in_specs=(
            P("grp", "blk", None),
            P("grp", "blk", None, None, None),
            P("grp", "blk", None),
            P("grp", "blk"),
            P("grp", "blk", None, None),
        ),
        out_specs=P("grp", "blk", None),
        check_vma=False,
    )
```

profile of v0, /device:TPU:1, one launch (start us, length us, event | category | flops | bytes accessed | tf_op | source)
XLA Modules:
  0.0 261.9 jit_solution(1155358600882321074)
XLA Ops:
  6.5 0.0 copy-start
  6.5 0.0 copy-start.1
  6.5 0.0 all-gather.6.cloned.1.call-start
  6.5 0.8 iota_compare_fusion
  7.3 2.2 convert_reduce_fusion
  9.6 0.1 select_reduce_fusion
  9.7 1.9 multiply_convert_fusion.2
  11.5 0.0 all-gather.6.cloned.1.call-update
  11.6 1.3 copy.10
  12.9 7.6 %all-to-all-start = ((s32[16,1,1]{2,1,0:T(1,128)}), s32[16,1,1]{2,1,0:T(1,128)S(1)}, u32[]{:S(2)}, u32[]{:S(2)}) async-start(s32[16,1,1]{2,1,0:T(1,128)} %copy.10), calls=%async_computation | async-start | bytes 16384 | tf_op jit(solution)/shard_map/all_to_all | solution.py:37
  20.5 0.0 all-gather.8.cloned.1.call-start
  20.5 1.2 fusion.25
  21.7 4.4 %collective-permute-start = (bf16[256,256]{1,0:T(8,128)(2,1)S(1)}, bf16[256,256]{1,0:T(8,128)(2,1)S(1)}, u32[]{:S(2)}, u32[]{:S(2)}) collective-permute-start(bf16[256,256]{1,0:T(8,128)(2,1)S(1)} %get-tuple-element.9), channel_id=1, source_target_pairs={{0,16},{16,32},{32,48},{48,64},{64,80},{80,96},{96,112},{112,128},... | collective-permute-start | bytes 393224 | tf_op jit(solution)/shard_map/ppermute | solution.py:15
  26.1 1.9 collective-permute-start.1
  28.1 0.0 copy-done.1
  28.1 0.1 reshape.310
  28.2 0.0 copy-done
  28.2 0.0 all-to-all-done
  28.3 0.1 copy.11
  28.4 0.0 collective-permute-done
  28.4 4.0 %collective-permute-done.1 = bf16[256,256]{1,0:T(8,128)(2,1)S(1)} collective-permute-done((bf16[256,256]{1,0:T(8,128)(2,1)S(1)}, bf16[256,256]{1,0:T(8,128)(2,1)S(1)}, u32[]{:S(2)}, u32[]{:S(2)}) %collective-permute-start.1) | collective-permute-done | bytes 131104 | tf_op jit(solution)/shard_map/ppermute | solution.py:18
  32.5 51.4 %all-gather.6.cloned.1.call-done = bf16[16,4,128,256]{3,2,1,0:T(8,128)(2,1)} async-done(((bf16[1,4,128,256]{3,2,1,0:T(8,128)(2,1)}), bf16[16,4,128,256]{3,2,1,0:T(8,128)(2,1)}) %all-gather.6.cloned.1.call-update) | async-done | bytes 4194320 | tf_op jit(solution)/shard_map/all_gather | solution.py:44
  83.9 3.8 %gather_fusion = bf16[16,128,256]{2,1,0:T(8,128)(2,1)} fusion(bf16[16,4,128,256]{3,2,1,0:T(8,128)(2,1)} %all-gather.6.cloned.1.call-done, s32[16]{0:T(128)S(1)} %or_bitcast_fusion), kind=kCustom, calls=%fused_computation | custom fusion | bytes 2097280 | tf_op jit(solution)/shard_map/gather | solution.py:45
  87.6 1.4 pad_maximum_fusion
  89.0 2.8 %gather_fusion.1 = bf16[64,128,256]{2,1,0:T(8,128)(2,1)} fusion(bf16[24,128,256]{2,1,0:T(8,128)(2,1)S(1)} %pad_maximum_fusion, s32[1024]{0:T(1024)S(1)} %pad_clamp_fusion), kind=kCustom, calls=%fused_computation.1 | custom fusion | bytes 8388864 | tf_op jit(solution)/shard_map/gather | solution.py:47
  91.8 3.8 %fusion.28 = (f32[4,128]{1,0:T(4,128)S(1)}, f32[4,256,128,1]{1,2,3,0:T(8,128)S(1)}) fusion(f32[4,128,256]{2,1,0:T(8,128)S(1)} %bitcast.108, f32[4,128]{1,0:T(4,128)S(1)} %get-tuple-element.15, bf16[4,16,128,256]{3,2,1,0:T(8,128)(2,1)} %bitcast.114, pred[4,16]{1,0:T(4,128)(4,1)S(1)} %iota_compare_fusion, bf16[1,4,16,128,128]{4,3,2,1,0:T(8,128)(2,1)} %param.6), kind=kOutput, calls=%fused_computation.53 | convolution fusion | flops 539360768 | bytes 7344192 | tf_op jit(solution)/shard_map/rkij,rkjc->ric/dot_general | solution.py:48
  95.5 1.0 multiply_convert_fusion.1
  96.5 0.0 all-gather.8.cloned.1.call-update
  96.5 0.0 all-gather.10.cloned.1.call-start
  96.6 0.3 fusion.26
  96.9 3.7 %collective-permute-start.2 = (bf16[256,256]{1,0:T(8,128)(2,1)S(1)}, bf16[256,256]{1,0:T(8,128)(2,1)S(1)}, u32[]{:S(2)}, u32[]{:S(2)}) collective-permute-start(bf16[256,256]{1,0:T(8,128)(2,1)S(1)} %get-tuple-element.7), channel_id=1, source_target_pairs={{0,16},{16,32},{32,48},{48,64},{64,80},{80,96},{96,112},{112,128},... | collective-permute-start | bytes 393224 | tf_op jit(solution)/shard_map/ppermute | solution.py:15
  100.6 1.9 collective-permute-start.3
  102.6 0.0 collective-permute-done.2
  102.6 4.3 %collective-permute-done.3 = bf16[256,256]{1,0:T(8,128)(2,1)S(1)} collective-permute-done((bf16[256,256]{1,0:T(8,128)(2,1)S(1)}, bf16[256,256]{1,0:T(8,128)(2,1)S(1)}, u32[]{:S(2)}, u32[]{:S(2)}) %collective-permute-start.3) | collective-permute-done | bytes 131104 | tf_op jit(solution)/shard_map/ppermute | solution.py:18
  107.0 56.3 %all-gather.8.cloned.1.call-done = bf16[64,128,256]{2,1,0:T(8,128)(2,1)} async-done(((bf16[4,128,256]{2,1,0:T(8,128)(2,1)}), bf16[64,128,256]{2,1,0:T(8,128)(2,1)}) %all-gather.8.cloned.1.call-update) | async-done | bytes 4194320 | tf_op jit(solution)/shard_map/all_gather | solution.py:44
  163.3 3.8 %gather_fusion.2 = bf16[16,128,256]{2,1,0:T(8,128)(2,1)} fusion(bf16[16,4,128,256]{3,2,1,0:T(8,128)(2,1)} %bitcast.120, s32[16]{0:T(128)S(1)} %or_bitcast_fusion), kind=kCustom, calls=%fused_computation.2 | custom fusion | bytes 2097280 | tf_op jit(solution)/shard_map/gather | solution.py:45
  167.1 1.4 pad_maximum_fusion.1
  168.4 2.8 %gather_fusion.3 = bf16[64,128,256]{2,1,0:T(8,128)(2,1)} fusion(bf16[24,128,256]{2,1,0:T(8,128)(2,1)S(1)} %pad_maximum_fusion.1, s32[1024]{0:T(1024)S(1)} %pad_clamp_fusion), kind=kCustom, calls=%fused_computation.3 | custom fusion | bytes 8388864 | tf_op jit(solution)/shard_map/gather | solution.py:47
  171.2 3.8 %fusion.29 = (f32[4,128]{1,0:T(4,128)S(1)}, f32[4,256,128,1]{1,2,3,0:T(8,128)S(1)}) fusion(f32[4,128,256]{2,1,0:T(8,128)S(1)} %bitcast.110, f32[4,128]{1,0:T(4,128)S(1)} %get-tuple-element.15, bf16[4,16,128,256]{3,2,1,0:T(8,128)(2,1)} %bitcast.115, pred[4,16]{1,0:T(4,128)(4,1)S(1)} %iota_compare_fusion, bf16[1,4,16,128,128]{4,3,2,1,0:T(8,128)(2,1)} %param.6), kind=kOutput, calls=%fused_computation.54 | convolution fusion | flops 539360768 | bytes 7344192 | tf_op jit(solution)/shard_map/rkij,rkjc->ric/dot_general | solution.py:48
  175.0 1.0 multiply_convert_fusion
  176.0 0.0 all-gather.10.cloned.1.call-update
  176.0 0.3 fusion.27
  176.3 3.7 %collective-permute-start.4 = (bf16[256,256]{1,0:T(8,128)(2,1)S(1)}, bf16[256,256]{1,0:T(8,128)(2,1)S(1)}, u32[]{:S(2)}, u32[]{:S(2)}) collective-permute-start(bf16[256,256]{1,0:T(8,128)(2,1)S(1)} %get-tuple-element.5), channel_id=1, source_target_pairs={{0,16},{16,32},{32,48},{48,64},{64,80},{80,96},{96,112},{112,128},... | collective-permute-start | bytes 393224 | tf_op jit(solution)/shard_map/ppermute | solution.py:15
  180.0 1.9 collective-permute-start.5
  182.0 0.0 collective-permute-done.4
  182.0 4.3 %collective-permute-done.5 = bf16[256,256]{1,0:T(8,128)(2,1)S(1)} collective-permute-done((bf16[256,256]{1,0:T(8,128)(2,1)S(1)}, bf16[256,256]{1,0:T(8,128)(2,1)S(1)}, u32[]{:S(2)}, u32[]{:S(2)}) %collective-permute-start.5) | collective-permute-done | bytes 131104 | tf_op jit(solution)/shard_map/ppermute | solution.py:18
  186.4 56.4 %all-gather.10.cloned.1.call-done = bf16[64,128,256]{2,1,0:T(8,128)(2,1)} async-done(((bf16[4,128,256]{2,1,0:T(8,128)(2,1)}), bf16[64,128,256]{2,1,0:T(8,128)(2,1)}) %all-gather.10.cloned.1.call-update) | async-done | bytes 4194320 | tf_op jit(solution)/shard_map/all_gather | solution.py:44
  242.8 3.8 %gather_fusion.4 = bf16[16,128,256]{2,1,0:T(8,128)(2,1)} fusion(bf16[16,4,128,256]{3,2,1,0:T(8,128)(2,1)} %bitcast.121, s32[16]{0:T(128)S(1)} %or_bitcast_fusion), kind=kCustom, calls=%fused_computation.4 | custom fusion | bytes 2097280 | tf_op jit(solution)/shard_map/gather | solution.py:45
  246.5 1.4 pad_maximum_fusion.2
  247.9 2.8 %gather_fusion.5 = bf16[64,128,256]{2,1,0:T(8,128)(2,1)} fusion(bf16[24,128,256]{2,1,0:T(8,128)(2,1)S(1)} %pad_maximum_fusion.2, s32[1024]{0:T(1024)S(1)} %pad_clamp_fusion), kind=kCustom, calls=%fused_computation.5 | custom fusion | bytes 8388864 | tf_op jit(solution)/shard_map/gather | solution.py:47
  250.6 3.7 %fusion.22 = (f32[4,128]{1,0:T(4,128)S(1)}, f32[4,256,128,1]{1,2,3,0:T(8,128)S(1)}) fusion(f32[4,128,256]{2,1,0:T(8,128)S(1)} %bitcast.112, f32[4,128]{1,0:T(4,128)S(1)} %get-tuple-element.15, bf16[4,16,128,256]{3,2,1,0:T(8,128)(2,1)} %bitcast.113, pred[4,16]{1,0:T(4,128)(4,1)S(1)} %iota_compare_fusion, bf16[1,4,16,128,128]{4,3,2,1,0:T(8,128)(2,1)} %param.6), kind=kOutput, calls=%fused_computation.38 | convolution fusion | flops 539360768 | bytes 7344192 | tf_op jit(solution)/shard_map/rkij,rkjc->ric/dot_general | solution.py:48
  254.4 1.0 add_divide_fusion
  (18 shorter events, 0.3 us)
Async XLA Ops:
  6.5 21.6 %copy-start = (f32[1,512,256]{2,1,0:T(8,128)S(1)}, f32[1,512,256]{2,1,0:T(8,128)}, u32[]{:S(2)}) copy-start(f32[1,512,256]{2,1,0:T(8,128)} %param.5) | copy-start | bytes 1572868
  6.5 21.5 %copy-start.1 = (s32[1,4,16]{2,1,0:T(4,128)S(1)}, s32[1,4,16]{2,1,0:T(4,128)}, u32[]{:S(2)}) copy-start(s32[1,4,16]{2,1,0:T(4,128)} %param.7) | copy-start | bytes 772
  6.5 77.3 %all-gather.6.cloned.1.call-start = ((), (), s32[]{:S(2)}) async-start(), calls=%async_computation.1 | async-start | bytes 4456448 | tf_op jit(solution)/shard_map/all_gather | solution.py:44
  12.9 15.4 %all-to-all-start = ((s32[16,1,1]{2,1,0:T(1,128)}), s32[16,1,1]{2,1,0:T(1,128)S(1)}, u32[]{:S(2)}, u32[]{:S(2)}) async-start(s32[16,1,1]{2,1,0:T(1,128)} %copy.10), calls=%async_computation | async-start | bytes 16384 | tf_op jit(solution)/shard_map/all_to_all | solution.py:37
  20.5 142.8 %all-gather.8.cloned.1.call-start = ((), (), s32[]{:S(2)}) async-start(), calls=%async_computation.2 | async-start | bytes 4456448 | tf_op jit(solution)/shard_map/all_gather | solution.py:44
  21.7 6.6 %collective-permute-start = (bf16[256,256]{1,0:T(8,128)(2,1)S(1)}, bf16[256,256]{1,0:T(8,128)(2,1)S(1)}, u32[]{:S(2)}, u32[]{:S(2)}) collective-permute-start(bf16[256,256]{1,0:T(8,128)(2,1)S(1)} %get-tuple-element.9), channel_id=1, source_target_pairs={{0,16},{16,32},{32,48},{48,64},{64,80},{80,96},{96,112},{112,128},... | collective-permute-start | bytes 393224 | tf_op jit(solution)/shard_map/ppermute | solution.py:15
  26.1 6.3 %collective-permute-start.1 = (bf16[256,256]{1,0:T(8,128)(2,1)S(1)}, bf16[256,256]{1,0:T(8,128)(2,1)S(1)}, u32[]{:S(2)}, u32[]{:S(2)}) collective-permute-start(bf16[256,256]{1,0:T(8,128)(2,1)S(1)} %get-tuple-element.10), channel_id=1, source_target_pairs={{16,0},{32,16},{48,32},{64,48},{80,64},{96,80},{112,96},{128,112},... | collective-permute-start | bytes 393224 | tf_op jit(solution)/shard_map/ppermute | solution.py:18
  96.5 146.2 %all-gather.10.cloned.1.call-start = ((), (), s32[]{:S(2)}) async-start(), calls=%async_computation.3 | async-start | bytes 4456448 | tf_op jit(solution)/shard_map/all_gather | solution.py:44
  96.9 5.7 %collective-permute-start.2 = (bf16[256,256]{1,0:T(8,128)(2,1)S(1)}, bf16[256,256]{1,0:T(8,128)(2,1)S(1)}, u32[]{:S(2)}, u32[]{:S(2)}) collective-permute-start(bf16[256,256]{1,0:T(8,128)(2,1)S(1)} %get-tuple-element.7), channel_id=1, source_target_pairs={{0,16},{16,32},{32,48},{48,64},{64,80},{80,96},{96,112},{112,128},... | collective-permute-start | bytes 393224 | tf_op jit(solution)/shard_map/ppermute | solution.py:15
  100.6 6.3 %collective-permute-start.3 = (bf16[256,256]{1,0:T(8,128)(2,1)S(1)}, bf16[256,256]{1,0:T(8,128)(2,1)S(1)}, u32[]{:S(2)}, u32[]{:S(2)}) collective-permute-start(bf16[256,256]{1,0:T(8,128)(2,1)S(1)} %get-tuple-element.8), channel_id=1, source_target_pairs={{16,0},{32,16},{48,32},{64,48},{80,64},{96,80},{112,96},{128,112},... | collective-permute-start | bytes 393224 | tf_op jit(solution)/shard_map/ppermute | solution.py:18
  176.3 5.7 %collective-permute-start.4 = (bf16[256,256]{1,0:T(8,128)(2,1)S(1)}, bf16[256,256]{1,0:T(8,128)(2,1)S(1)}, u32[]{:S(2)}, u32[]{:S(2)}) collective-permute-start(bf16[256,256]{1,0:T(8,128)(2,1)S(1)} %get-tuple-element.5), channel_id=1, source_target_pairs={{0,16},{16,32},{32,48},{48,64},{64,80},{80,96},{96,112},{112,128},... | collective-permute-start | bytes 393224 | tf_op jit(solution)/shard_map/ppermute | solution.py:15
  180.0 6.3 %collective-permute-start.5 = (bf16[256,256]{1,0:T(8,128)(2,1)S(1)}, bf16[256,256]{1,0:T(8,128)(2,1)S(1)}, u32[]{:S(2)}, u32[]{:S(2)}) collective-permute-start(bf16[256,256]{1,0:T(8,128)(2,1)S(1)} %get-tuple-element.6), channel_id=1, source_target_pairs={{16,0},{32,16},{48,32},{64,48},{80,64},{96,80},{112,96},{128,112},... | collective-permute-start | bytes 393224 | tf_op jit(solution)/shard_map/ppermute | solution.py:18
Sparse Core Ops, SparseCore 0:
  11.7 72.1 all-gather.5
  96.6 66.6 all-gather.7
  176.1 66.6 all-gather.9
where the time goes:
time: 263 us; the launch traced here: 262 us
  waiting for transfers between devices  177 us (67%)
  starting transfers between devices  25.3 us (10%)
  local copies, waits for them, and re-layouts  21.1 us (8%)
  other arithmetic  14 us (5%)
  between operations  13.3 us (5%)
  matrix products  11.3 us (4%)
    all_gather x3, waiting for transfers between devices, on_device(): copies = lax.all_gather(own_blocks[None], 'grp', axis=0, tiled=True)  164 us
    ppermute x3, waiting for transfers between devices, with_halo(): lax.ppermute(lax.slice_in_dim(block, 0, width, axis=dim), axis, backward)  12.7 us
    ppermute x3, starting transfers between devices, with_halo(): lax.ppermute(lax.slice_in_dim(block, block.shape[dim] - width, None, axis...  11.9 us
    gather x3, local copies, waits for them, and re-layouts, on_device(): cross = copies[band_ids[:, None], arrived]  11.3 us
    dot_general x3, matrix products, on_device(): jnp.einsum('rkij,rkjc->ric', tiles[0], chosen, preferred_element_type=jnp...  11.3 us
    gather x3, local copies, waits for them, and re-layouts, on_device(): ext[tile_cols[0]]  8.28 us
    all_to_all x1, starting transfers between devices, on_device(): lax.all_to_all(picks, 'grp', split_axis=0, concat_axis=0, tiled=True)  7.58 us
    ppermute x3, starting transfers between devices, with_halo(): lax.ppermute(lax.slice_in_dim(block, 0, width, axis=dim), axis, backward)  5.76 us
  transfers between devices with their start and end apart: 10, of which 6 were waited for; matrix products, arithmetic and copies ran while one was open for 1% of the time, Pallas kernels for 0%

commit v1 on v0

--- a/solution.py
+++ b/solution.py
@@ -41,7 +41,10 @@
         padded = with_halo(scaled, (("blk", 0),), HB * bsize)
         local = padded.reshape(n_rows + 2 * HB, bsize, classes)
         own_blocks = scaled.reshape(n_rows, bsize, classes)
-        copies = lax.all_gather(own_blocks[None], "grp", axis=0, tiled=True)
+        copies = jnp.concatenate(
+            lax.all_to_all(jnp.stack([own_blocks[None]] * lax.axis_size("grp")), "grp", 0, 0),
+            axis=0,
+        )
         cross = copies[band_ids[:, None], arrived]
         ext = jnp.concatenate([local, cross.reshape(-1, bsize, classes)], axis=0)
         chosen = jnp.where(valid[..., None, None], ext[tile_cols[0]], jnp.zeros((), jnp.bfloat16))

time: 263 us -> 243 us (0.924)
  the two profiles are of different devices: /device:TPU:1 before, /device:TPU:288 now
where the time goes in v1:
time: 243 us; the launch traced here: 242 us
  waiting for transfers between devices  155 us (64%)
  starting transfers between devices  37.5 us (15%)
  local copies, waits for them, and re-layouts  25.7 us (11%)
  other arithmetic  12.5 us (5%)
  matrix products  11.2 us (5%)
    all_to_all x3, waiting for transfers between devices, on_device(): lax.all_to_all(jnp.stack([own_blocks[None]] * lax.axis_size('grp')), 'grp...  144 us
    all_to_all x3, starting transfers between devices, on_device(): lax.all_to_all(jnp.stack([own_blocks[None]] * lax.axis_size('grp')), 'grp...  13.8 us
    dot_general x3, matrix products, on_device(): jnp.einsum('rkij,rkjc->ric', tiles[0], chosen, preferred_element_type=jnp...  11.2 us
    ppermute x3, starting transfers between devices, with_halo(): lax.ppermute(lax.slice_in_dim(block, 0, width, axis=dim), axis, backward)  10.9 us
    gather x3, local copies, waits for them, and re-layouts, on_device(): cross = copies[band_ids[:, None], arrived]  8.41 us
    gather x3, local copies, waits for them, and re-layouts, on_device(): ext[tile_cols[0]]  8.29 us
    another operation x3, local copies, waits for them, and re-layouts, on_device(): jnp.stack([own_blocks[None]] * lax.axis_size('grp'))  7.44 us
    all_to_all x1, starting transfers between devices, on_device(): lax.all_to_all(picks, 'grp', split_axis=0, concat_axis=0, tiled=True)  7.03 us
  transfers between devices with their start and end apart: 10, of which 10 were waited for; matrix products, arithmetic and copies ran while one was open for 3% of the time, Pallas kernels for 0%

profile of v1, /device:TPU:288, one launch (start us, length us, event | category | flops | bytes accessed | tf_op | source)
XLA Modules:
  0.0 242.3 jit_solution(4795149982236787539)
XLA Ops:
  0.0 1.3 copy.10
  1.3 7.0 %all-to-all-start.1 = ((s32[16,1,1]{2,1,0:T(1,128)}), s32[16,1,1]{2,1,0:T(1,128)S(1)}, u32[]{:S(2)}, u32[]{:S(2)}) async-start(s32[16,1,1]{2,1,0:T(1,128)} %copy.10), calls=%async_computation.1 | async-start | bytes 16384 | tf_op jit(solution)/shard_map/all_to_all | solution.py:37
  8.4 0.7 iota_compare_fusion
  9.1 2.2 convert_reduce_fusion
  11.3 0.1 select_reduce_fusion
  11.4 1.2 multiply_convert_fusion.2
  12.6 3.2 %all-to-all-done.1 = s32[16,1,1]{2,1,0:T(1,128)S(1)} async-done(((s32[16,1,1]{2,1,0:T(1,128)}), s32[16,1,1]{2,1,0:T(1,128)S(1)}, u32[]{:S(2)}, u32[]{:S(2)}) %all-to-all-start.1) | async-done | bytes 96 | tf_op jit(solution)/shard_map/all_to_all | solution.py:37
  15.9 2.5 %stack.9 = bf16[16,1,4,128,256]{4,3,2,1,0:T(8,128)(2,1)} broadcast(bf16[4,128,256]{2,1,0:T(8,128)(2,1)S(1)} %multiply_convert_fusion.2), dimensions={2,3,4} | broadcast | bytes 4456448 | tf_op jit(solution)/shard_map/stack | solution.py:45
  18.3 0.0 copy-start
  18.3 0.0 copy-start.1
  18.3 4.7 %all-to-all-start = ((bf16[16,1,4,128,256]{4,3,2,1,0:T(8,128)(2,1)}), bf16[16,1,4,128,256]{4,3,2,1,0:T(8,128)(2,1)}, u32[]{:S(2)}, u32[]{:S(2)}) async-start(bf16[16,1,4,128,256]{4,3,2,1,0:T(8,128)(2,1)} %stack.9), calls=%async_computation | async-start | bytes 8388608 | tf_op jit(solution)/shard_map/all_to_all | solution.py:45
  23.0 0.0 copy-done
  23.0 0.1 fusion.25
  23.2 1.9 collective-permute-start
  25.1 3.6 %collective-permute-start.1 = (bf16[256,256]{1,0:T(8,128)(2,1)S(1)}, bf16[256,256]{1,0:T(8,128)(2,1)S(1)}, u32[]{:S(2)}, u32[]{:S(2)}) collective-permute-start(bf16[256,256]{1,0:T(8,128)(2,1)S(1)} %get-tuple-element.10), channel_id=1, source_target_pairs={{16,0},{32,16},{48,32},{64,48},{80,64},{96,80},{112,96},{128,112},... | collective-permute-start | bytes 393224 | tf_op jit(solution)/shard_map/ppermute | solution.py:18
  28.8 0.0 copy-done.1
  28.8 0.1 reshape.333
  28.9 0.1 copy.11
  29.0 0.5 collective-permute-done
  29.5 1.8 collective-permute-done.1
  31.3 0.8 pad_maximum_fusion.3
  32.1 51.2 %all-to-all-done = bf16[16,1,4,128,256]{4,3,2,1,0:T(8,128)(2,1)} async-done(((bf16[16,1,4,128,256]{4,3,2,1,0:T(8,128)(2,1)}), bf16[16,1,4,128,256]{4,3,2,1,0:T(8,128)(2,1)}, u32[]{:S(2)}, u32[]{:S(2)}) %all-to-all-start) | async-done | bytes 4194336 | tf_op jit(solution)/shard_map/all_to_all | solution.py:45
  83.4 2.8 %gather_fusion = bf16[16,128,256]{2,1,0:T(8,128)(2,1)S(1)} fusion(bf16[16,4,128,256]{3,2,1,0:T(8,128)(2,1)} %bitcast.6, s32[16]{0:T(128)S(1)} %or_bitcast_fusion), kind=kCustom, calls=%fused_computation | custom fusion | bytes 2097280 | tf_op jit(solution)/shard_map/gather | solution.py:48
  86.2 1.2 pad_maximum_fusion
  87.4 2.8 %gather_fusion.1 = bf16[64,128,256]{2,1,0:T(8,128)(2,1)} fusion(bf16[24,128,256]{2,1,0:T(8,128)(2,1)S(1)} %pad_maximum_fusion, s32[1024]{0:T(1024)S(1)} %pad_clamp_fusion), kind=kCustom, calls=%fused_computation.1 | custom fusion | bytes 8388864 | tf_op jit(solution)/shard_map/gather | solution.py:50
  90.1 3.7 %fusion.28 = (f32[4,128]{1,0:T(4,128)S(1)}, f32[4,256,128,1]{1,2,3,0:T(8,128)S(1)}) fusion(f32[4,128,256]{2,1,0:T(8,128)S(1)} %bitcast.108, f32[4,128]{1,0:T(4,128)S(1)} %get-tuple-element.15, bf16[4,16,128,256]{3,2,1,0:T(8,128)(2,1)} %bitcast.114, pred[4,16]{1,0:T(4,128)(4,1)S(1)} %iota_compare_fusion, bf16[1,4,16,128,128]{4,3,2,1,0:T(8,128)(2,1)} %param.6), kind=kOutput, calls=%fused_computation.52 | convolution fusion | flops 539491840 | bytes 7344192 | tf_op jit(solution)/shard_map/rkij,rkjc->ric/dot_general | solution.py:51
  93.9 0.3 multiply_convert_fusion.1
  94.2 2.5 %stack.10 = bf16[16,1,4,128,256]{4,3,2,1,0:T(8,128)(2,1)} broadcast(bf16[4,128,256]{2,1,0:T(8,128)(2,1)S(1)} %multiply_convert_fusion.1), dimensions={2,3,4} | broadcast | bytes 4456448 | tf_op jit(solution)/shard_map/stack | solution.py:45
  96.6 4.6 %all-to-all-start.2 = ((bf16[16,1,4,128,256]{4,3,2,1,0:T(8,128)(2,1)}), bf16[16,1,4,128,256]{4,3,2,1,0:T(8,128)(2,1)}, u32[]{:S(2)}, u32[]{:S(2)}) async-start(bf16[16,1,4,128,256]{4,3,2,1,0:T(8,128)(2,1)} %stack.10), calls=%async_computation.2 | async-start | bytes 8388608 | tf_op jit(solution)/shard_map/all_to_all | solution.py:45
  101.2 0.3 fusion.26
  101.5 1.9 collective-permute-start.2
  103.4 3.6 %collective-permute-start.3 = (bf16[256,256]{1,0:T(8,128)(2,1)S(1)}, bf16[256,256]{1,0:T(8,128)(2,1)S(1)}, u32[]{:S(2)}, u32[]{:S(2)}) collective-permute-start(bf16[256,256]{1,0:T(8,128)(2,1)S(1)} %get-tuple-element.8), channel_id=1, source_target_pairs={{16,0},{32,16},{48,32},{64,48},{80,64},{96,80},{112,96},{128,112},... | collective-permute-start | bytes 393224 | tf_op jit(solution)/shard_map/ppermute | solution.py:18
  107.1 0.7 collective-permute-done.2
  107.8 1.8 collective-permute-done.3
  109.6 0.8 pad_maximum_fusion.4
  110.4 48.3 %all-to-all-done.2 = bf16[16,1,4,128,256]{4,3,2,1,0:T(8,128)(2,1)} async-done(((bf16[16,1,4,128,256]{4,3,2,1,0:T(8,128)(2,1)}), bf16[16,1,4,128,256]{4,3,2,1,0:T(8,128)(2,1)}, u32[]{:S(2)}, u32[]{:S(2)}) %all-to-all-start.2) | async-done | bytes 4194336 | tf_op jit(solution)/shard_map/all_to_all | solution.py:45
  158.7 2.8 %gather_fusion.2 = bf16[16,128,256]{2,1,0:T(8,128)(2,1)S(1)} fusion(bf16[16,4,128,256]{3,2,1,0:T(8,128)(2,1)} %bitcast.19, s32[16]{0:T(128)S(1)} %or_bitcast_fusion), kind=kCustom, calls=%fused_computation.2 | custom fusion | bytes 2097280 | tf_op jit(solution)/shard_map/gather | solution.py:48
  161.5 1.2 pad_maximum_fusion.1
  162.7 2.8 %gather_fusion.3 = bf16[64,128,256]{2,1,0:T(8,128)(2,1)} fusion(bf16[24,128,256]{2,1,0:T(8,128)(2,1)S(1)} %pad_maximum_fusion.1, s32[1024]{0:T(1024)S(1)} %pad_clamp_fusion), kind=kCustom, calls=%fused_computation.3 | custom fusion | bytes 8388864 | tf_op jit(solution)/shard_map/gather | solution.py:50
  165.5 3.7 %fusion.29 = (f32[4,128]{1,0:T(4,128)S(1)}, f32[4,256,128,1]{1,2,3,0:T(8,128)S(1)}) fusion(f32[4,128,256]{2,1,0:T(8,128)S(1)} %bitcast.110, f32[4,128]{1,0:T(4,128)S(1)} %get-tuple-element.15, bf16[4,16,128,256]{3,2,1,0:T(8,128)(2,1)} %bitcast.115, pred[4,16]{1,0:T(4,128)(4,1)S(1)} %iota_compare_fusion, bf16[1,4,16,128,128]{4,3,2,1,0:T(8,128)(2,1)} %param.6), kind=kOutput, calls=%fused_computation.53 | convolution fusion | flops 539491840 | bytes 7344192 | tf_op jit(solution)/shard_map/rkij,rkjc->ric/dot_general | solution.py:51
  169.2 0.3 multiply_convert_fusion
  169.5 2.5 %stack.11 = bf16[16,1,4,128,256]{4,3,2,1,0:T(8,128)(2,1)} broadcast(bf16[4,128,256]{2,1,0:T(8,128)(2,1)S(1)} %multiply_convert_fusion), dimensions={2,3,4} | broadcast | bytes 4456448 | tf_op jit(solution)/shard_map/stack | solution.py:45
  172.0 4.6 %all-to-all-start.3 = ((bf16[16,1,4,128,256]{4,3,2,1,0:T(8,128)(2,1)}), bf16[16,1,4,128,256]{4,3,2,1,0:T(8,128)(2,1)}, u32[]{:S(2)}, u32[]{:S(2)}) async-start(bf16[16,1,4,128,256]{4,3,2,1,0:T(8,128)(2,1)} %stack.11), calls=%async_computation.3 | async-start | bytes 8388608 | tf_op jit(solution)/shard_map/all_to_all | solution.py:45
  176.5 0.3 fusion.27
  176.8 1.9 collective-permute-start.4
  178.8 3.6 %collective-permute-start.5 = (bf16[256,256]{1,0:T(8,128)(2,1)S(1)}, bf16[256,256]{1,0:T(8,128)(2,1)S(1)}, u32[]{:S(2)}, u32[]{:S(2)}) collective-permute-start(bf16[256,256]{1,0:T(8,128)(2,1)S(1)} %get-tuple-element.6), channel_id=1, source_target_pairs={{16,0},{32,16},{48,32},{64,48},{80,64},{96,80},{112,96},{128,112},... | collective-permute-start | bytes 393224 | tf_op jit(solution)/shard_map/ppermute | solution.py:18
  182.4 0.7 collective-permute-done.4
  183.1 1.8 collective-permute-done.5
  184.9 0.8 pad_maximum_fusion.5
  185.8 45.0 %all-to-all-done.3 = bf16[16,1,4,128,256]{4,3,2,1,0:T(8,128)(2,1)} async-done(((bf16[16,1,4,128,256]{4,3,2,1,0:T(8,128)(2,1)}), bf16[16,1,4,128,256]{4,3,2,1,0:T(8,128)(2,1)}, u32[]{:S(2)}, u32[]{:S(2)}) %all-to-all-start.3) | async-done | bytes 4194336 | tf_op jit(solution)/shard_map/all_to_all | solution.py:45
  230.7 2.8 %gather_fusion.4 = bf16[16,128,256]{2,1,0:T(8,128)(2,1)S(1)} fusion(bf16[16,4,128,256]{3,2,1,0:T(8,128)(2,1)} %bitcast.28, s32[16]{0:T(128)S(1)} %or_bitcast_fusion), kind=kCustom, calls=%fused_computation.4 | custom fusion | bytes 2097280 | tf_op jit(solution)/shard_map/gather | solution.py:48
  233.5 1.2 pad_maximum_fusion.2
  234.7 2.8 %gather_fusion.5 = bf16[64,128,256]{2,1,0:T(8,128)(2,1)} fusion(bf16[24,128,256]{2,1,0:T(8,128)(2,1)S(1)} %pad_maximum_fusion.2, s32[1024]{0:T(1024)S(1)} %pad_clamp_fusion), kind=kCustom, calls=%fused_computation.5 | custom fusion | bytes 8388864 | tf_op jit(solution)/shard_map/gather | solution.py:50
  237.5 3.8 %fusion.22 = (f32[4,128]{1,0:T(4,128)S(1)}, f32[4,256,128,1]{1,2,3,0:T(8,128)S(1)}) fusion(f32[4,128,256]{2,1,0:T(8,128)S(1)} %bitcast.112, f32[4,128]{1,0:T(4,128)S(1)} %get-tuple-element.15, bf16[4,16,128,256]{3,2,1,0:T(8,128)(2,1)} %bitcast.113, pred[4,16]{1,0:T(4,128)(4,1)S(1)} %iota_compare_fusion, bf16[1,4,16,128,128]{4,3,2,1,0:T(8,128)(2,1)} %param.6), kind=kOutput, calls=%fused_computation.38 | convolution fusion | flops 539491840 | bytes 7344192 | tf_op jit(solution)/shard_map/rkij,rkjc->ric/dot_general | solution.py:51
  241.3 1.0 add_divide_fusion
  (14 shorter events, 0.1 us)
Async XLA Ops:
  1.3 14.5 %all-to-all-start.1 = ((s32[16,1,1]{2,1,0:T(1,128)}), s32[16,1,1]{2,1,0:T(1,128)S(1)}, u32[]{:S(2)}, u32[]{:S(2)}) async-start(s32[16,1,1]{2,1,0:T(1,128)} %copy.10), calls=%async_computation.1 | async-start | bytes 16384 | tf_op jit(solution)/shard_map/all_to_all | solution.py:37
  18.3 4.7 %copy-start = (f32[1,512,256]{2,1,0:T(8,128)S(1)}, f32[1,512,256]{2,1,0:T(8,128)}, u32[]{:S(2)}) copy-start(f32[1,512,256]{2,1,0:T(8,128)} %param.5) | copy-start | bytes 1572868
  18.3 10.5 %copy-start.1 = (s32[1,4,16]{2,1,0:T(4,128)S(1)}, s32[1,4,16]{2,1,0:T(4,128)}, u32[]{:S(2)}) copy-start(s32[1,4,16]{2,1,0:T(4,128)} %param.7) | copy-start | bytes 772
  18.3 65.0 %all-to-all-start = ((bf16[16,1,4,128,256]{4,3,2,1,0:T(8,128)(2,1)}), bf16[16,1,4,128,256]{4,3,2,1,0:T(8,128)(2,1)}, u32[]{:S(2)}, u32[]{:S(2)}) async-start(bf16[16,1,4,128,256]{4,3,2,1,0:T(8,128)(2,1)} %stack.9), calls=%async_computation | async-start | bytes 8388608 | tf_op jit(solution)/shard_map/all_to_all | solution.py:45
  23.2 6.3 %collective-permute-start = (bf16[256,256]{1,0:T(8,128)(2,1)S(1)}, bf16[256,256]{1,0:T(8,128)(2,1)S(1)}, u32[]{:S(2)}, u32[]{:S(2)}) collective-permute-start(bf16[256,256]{1,0:T(8,128)(2,1)S(1)} %get-tuple-element.9), channel_id=1, source_target_pairs={{0,16},{16,32},{32,48},{48,64},{64,80},{80,96},{96,112},{112,128},... | collective-permute-start | bytes 393224 | tf_op jit(solution)/shard_map/ppermute | solution.py:15
  25.1 6.1 %collective-permute-start.1 = (bf16[256,256]{1,0:T(8,128)(2,1)S(1)}, bf16[256,256]{1,0:T(8,128)(2,1)S(1)}, u32[]{:S(2)}, u32[]{:S(2)}) collective-permute-start(bf16[256,256]{1,0:T(8,128)(2,1)S(1)} %get-tuple-element.10), channel_id=1, source_target_pairs={{16,0},{32,16},{48,32},{64,48},{80,64},{96,80},{112,96},{128,112},... | collective-permute-start | bytes 393224 | tf_op jit(solution)/shard_map/ppermute | solution.py:18
  96.6 62.1 %all-to-all-start.2 = ((bf16[16,1,4,128,256]{4,3,2,1,0:T(8,128)(2,1)}), bf16[16,1,4,128,256]{4,3,2,1,0:T(8,128)(2,1)}, u32[]{:S(2)}, u32[]{:S(2)}) async-start(bf16[16,1,4,128,256]{4,3,2,1,0:T(8,128)(2,1)} %stack.10), calls=%async_computation.2 | async-start | bytes 8388608 | tf_op jit(solution)/shard_map/all_to_all | solution.py:45
  101.5 6.3 %collective-permute-start.2 = (bf16[256,256]{1,0:T(8,128)(2,1)S(1)}, bf16[256,256]{1,0:T(8,128)(2,1)S(1)}, u32[]{:S(2)}, u32[]{:S(2)}) collective-permute-start(bf16[256,256]{1,0:T(8,128)(2,1)S(1)} %get-tuple-element.7), channel_id=1, source_target_pairs={{0,16},{16,32},{32,48},{48,64},{64,80},{80,96},{96,112},{112,128},... | collective-permute-start | bytes 393224 | tf_op jit(solution)/shard_map/ppermute | solution.py:15
  103.4 6.1 %collective-permute-start.3 = (bf16[256,256]{1,0:T(8,128)(2,1)S(1)}, bf16[256,256]{1,0:T(8,128)(2,1)S(1)}, u32[]{:S(2)}, u32[]{:S(2)}) collective-permute-start(bf16[256,256]{1,0:T(8,128)(2,1)S(1)} %get-tuple-element.8), channel_id=1, source_target_pairs={{16,0},{32,16},{48,32},{64,48},{80,64},{96,80},{112,96},{128,112},... | collective-permute-start | bytes 393224 | tf_op jit(solution)/shard_map/ppermute | solution.py:18
  172.0 58.7 %all-to-all-start.3 = ((bf16[16,1,4,128,256]{4,3,2,1,0:T(8,128)(2,1)}), bf16[16,1,4,128,256]{4,3,2,1,0:T(8,128)(2,1)}, u32[]{:S(2)}, u32[]{:S(2)}) async-start(bf16[16,1,4,128,256]{4,3,2,1,0:T(8,128)(2,1)} %stack.11), calls=%async_computation.3 | async-start | bytes 8388608 | tf_op jit(solution)/shard_map/all_to_all | solution.py:45
  176.8 6.3 %collective-permute-start.4 = (bf16[256,256]{1,0:T(8,128)(2,1)S(1)}, bf16[256,256]{1,0:T(8,128)(2,1)S(1)}, u32[]{:S(2)}, u32[]{:S(2)}) collective-permute-start(bf16[256,256]{1,0:T(8,128)(2,1)S(1)} %get-tuple-element.5), channel_id=1, source_target_pairs={{0,16},{16,32},{32,48},{48,64},{64,80},{80,96},{96,112},{112,128},... | collective-permute-start | bytes 393224 | tf_op jit(solution)/shard_map/ppermute | solution.py:15
  178.8 6.1 %collective-permute-start.5 = (bf16[256,256]{1,0:T(8,128)(2,1)S(1)}, bf16[256,256]{1,0:T(8,128)(2,1)S(1)}, u32[]{:S(2)}, u32[]{:S(2)}) collective-permute-start(bf16[256,256]{1,0:T(8,128)(2,1)S(1)} %get-tuple-element.6), channel_id=1, source_target_pairs={{16,0},{32,16},{48,32},{64,48},{80,64},{96,80},{112,96},{128,112},... | collective-permute-start | bytes 393224 | tf_op jit(solution)/shard_map/ppermute | solution.py:18
